TPU v7x, 32 devices: a whole 2x2x4 slice. The times are simulated.
32 devices in a mesh: group: 2 (over y), dp: 16 (over z, x, core).
Axes of the slice: x: 2, y: 2, z: 4, core: 2. Of those that a mesh axis runs over, the one named last changes fastest.
Arguments:
- clips_feat: bfloat16 [4096, 4096], P(('group', 'dp')), parts along dimension 0, may hold values from -6 to 6
- weight: bfloat16 [4096, 384], P('dp'), may hold values from -0.09375 to 0.09375
- sentences: bfloat16 [4096, 384], P(('group', 'dp')), parts along dimension 0, may hold values from -6 to 6
- log_scale: float32 [1], replicated, may hold values from 4.3 to 4.6
- bias: float32 [1], replicated, may hold values from -14 to -11
- positives: int32 [4096, 2], P(('group', 'dp')), parts along dimension 0, may hold values from 0 to 2047
Outputs:
- clip_loss: float32 [4096], P(('group', 'dp')), parts along dimension 0
- grad_weight: float32 [8192, 384], P(('group', 'dp')), parts along dimension 0
- grad_scalars: float32 [4], P('group'), parts along dimension 0
There are 2 independent parts, one for each index of `group`. A program takes and returns all parts, laid end to end along the dimension named above; an argument that names none is the same for every part. Nothing has to cross between parts.
Inputs may be any that keep to these rules, and one draw needn't show every extreme that they name: `positives`: two sentence ids for each clip; they may coincide.
All inputs are finite; a program needn't handle non-finite values.
Results may differ from a plain program's by a relative error of at most 0.002.
The roundings to bfloat16 on the way count: a program that leaves them out, or rounds other values in their place, can miss the bound.
Values may be sent and summed in bfloat16 or wider, within the bound.
A program may use at most 64 MiB of HBM per device.

v0:
```python
import jax
import jax.numpy as jnp
from jax import lax
from jax.sharding import PartitionSpec as P

column_block = 2048


def swapped(x, axis, apart):
    return lax.ppermute(x, axis, [(i, i ^ 1 << apart) for i in range(lax.axis_size(axis))])


def shards(clips_feat, weight, sentences, log_scale, bias, positives):
    rows_here = clips_feat.shape[0]
    embed_width = weight.shape[1]
    devices = lax.axis_size("dp")
    position = lax.axis_index("dp")
    full_weight = lax.all_gather(weight, "dp", axis=0, tiled=True)
    proj = jnp.dot(clips_feat, full_weight, preferred_element_type=jnp.float32)
    inverse = lax.rsqrt(jnp.sum(proj * proj, axis=1, keepdims=True) + 1e-06)
    unit32 = proj * inverse
    clip_unit = unit32.astype(jnp.bfloat16)
    sent32 = sentences.astype(jnp.float32)
    sent_unit = (
        sent32 * lax.rsqrt(jnp.sum(sent32 * sent32, axis=1, keepdims=True) + 1e-06)
    ).astype(jnp.bfloat16)
    scale = jnp.exp(log_scale[0])
    shift = bias[0]
    inv_count = 1.0 / (rows_here * devices)
    first_pos = positives[:, 0:1]
    second_pos = positives[:, 1:2]

    def one_tile(carry, block, start):
        losses, grad, dscale, dbias = carry
        span = block.shape[0]
        products = lax.dot_general(
            clip_unit, block, (((1,), (1,)), ((), ())), preferred_element_type=jnp.float32
        )
        logits = scale * products + shift
        columns = start + lax.iota(jnp.int32, span)
        matched = (first_pos == columns[None, :]) | (second_pos == columns[None, :])
        target = jnp.where(matched, jnp.float32(1.0), jnp.float32(-1.0))
        margin = target * logits
        losses = losses - jnp.sum(jax.nn.log_sigmoid(margin), axis=1)
        grad_logit = -target * jax.nn.sigmoid(-margin) * inv_count
        dscale = dscale + jnp.sum(grad_logit * (scale * products))
        dbias = dbias + jnp.sum(grad_logit)
        grad = grad + jnp.dot(
            grad_logit.astype(jnp.bfloat16), block, preferred_element_type=jnp.float32
        )
        return (losses, grad, dscale, dbias)

    def tile_rows(carry, piece, start):
        span = piece.shape[0]
        if span > column_block and span % column_block == 0:
            stacked = piece.reshape(span // column_block, column_block, embed_width)
            offsets = start + column_block * lax.iota(jnp.int32, span // column_block)

            def step_once(inner_carry, inputs):
                return (one_tile(inner_carry, inputs[0], inputs[1]), None)

            result, unused = lax.scan(step_once, carry, (stacked, offsets))
            return result
        return one_tile(carry, piece, start)

    initial = (
        jnp.zeros((rows_here,), jnp.float32),
        jnp.zeros((rows_here, embed_width), jnp.float32),
        jnp.float32(0.0),
        jnp.float32(0.0),
    )
    carry = tile_rows(initial, sent_unit, position * rows_here)
    buffer = sent_unit
    levels = devices.bit_length() - 1
    for level in range(levels):
        other = swapped(buffer, "dp", level)
        stride = 1 << level
        partner_base = jnp.bitwise_xor(position, stride) // stride * stride
        carry = tile_rows(carry, other, partner_base * rows_here)
        if level + 1 < levels:
            upper = position // stride % 2 == 1
            buffer = jnp.where(
                upper,
                jnp.concatenate([other, buffer], axis=0),
                jnp.concatenate([buffer, other], axis=0),
            )
    clip_loss, grad, dscale, dbias = carry
    grad_unit = scale * grad
    inner = jnp.sum(unit32 * grad_unit, axis=1, keepdims=True)
    grad_proj = (inverse * (grad_unit - unit32 * inner)).astype(jnp.bfloat16)
    grad_weight = lax.psum_scatter(
        lax.dot_general(
            clips_feat, grad_proj, (((0,), (0,)), ((), ())), preferred_element_type=jnp.float32
        ),
        "dp",
        scatter_dimension=0,
        tiled=True,
    )
    summed = lax.psum((dscale, dbias), "dp")
    grad_scalars = jnp.stack([summed[0], summed[1]])
    return (clip_loss, grad_weight, grad_scalars)


def solution(mesh):
    in_specs = (
        P(("group", "dp"), None),
        P("dp", None),
        P(("group", "dp"), None),
        P(),
        P(),
        P(("group", "dp"), None),
    )
    out_specs = (P(("group", "dp")), P(("group", "dp"), None), P("group"))
    return jax.shard_map(shards, mesh=mesh, in_specs=in_specs, out_specs=out_specs, check_vma=False)
```

profile of v0, /device:TPU:1, one launch (start us, length us, event | category | flops | bytes accessed | tf_op | source)
XLA Modules:
  0.0 190.5 jit_solution(283245672790788973)
XLA Ops:
  7.2 0.0 copy-start
  7.2 0.0 all-gather.2.cloned.1.call-start
  7.2 0.7 all-gather.2.cloned.1.call-update
  7.9 0.0 reduce-scatter.2.cloned.1.call-start
  8.0 1.0 fusion.12
  9.0 1.0 fusion.13
  10.0 0.1 collective-permute-start
  11.5 0.0 collective-permute-done
  11.6 2.6 %collective-permute-start.1 = (bf16[256,384]{1,0:T(8,128)(2,1)S(1)}, bf16[256,384]{1,0:T(8,128)(2,1)S(1)}, u32[]{:S(2)}, u32[]{:S(2)}) collective-permute-start(bf16[256,384]{1,0:T(8,128)(2,1)S(1)} %maximum_select_fusion.2), channel_id=1, source_target_pairs={{0,2},{1,3},{2,0},{3,1},{4,6},{5,7},{6,4},{7,5},{8,10},{9,11},{10,... | collective-permute-start | bytes 589832 | tf_op jit(solution)/shard_map/ppermute | solution.py:10
  14.2 5.1 %collective-permute-done.1 = bf16[256,384]{1,0:T(8,128)(2,1)S(1)} collective-permute-done((bf16[256,384]{1,0:T(8,128)(2,1)S(1)}, bf16[256,384]{1,0:T(8,128)(2,1)S(1)}, u32[]{:S(2)}, u32[]{:S(2)}) %collective-permute-start.1) | collective-permute-done | bytes 196640 | tf_op jit(solution)/shard_map/ppermute | solution.py:10
  19.4 0.1 maximum_select_fusion.1
  19.5 1.4 collective-permute-start.2
  20.9 0.8 slice_bitcast_fusion.1
  21.6 13.9 %collective-permute-done.2 = bf16[512,384]{1,0:T(8,128)(2,1)S(1)} collective-permute-done((bf16[512,384]{1,0:T(8,128)(2,1)S(1)}, bf16[512,384]{1,0:T(8,128)(2,1)S(1)}, u32[]{:S(2)}, u32[]{:S(2)}) %collective-permute-start.2) | collective-permute-done | bytes 393248 | tf_op jit(solution)/shard_map/ppermute | solution.py:10
  35.5 0.3 maximum_select_fusion
  35.9 2.9 %collective-permute-start.3 = (bf16[1024,384]{1,0:T(8,128)(2,1)S(1)}, bf16[1024,384]{1,0:T(8,128)(2,1)S(1)}, u32[]{:S(2)}, u32[]{:S(2)}) collective-permute-start(bf16[1024,384]{1,0:T(8,128)(2,1)S(1)} %maximum_select_fusion), channel_id=1, source_target_pairs={{0,8},{1,9},{2,10},{3,11},{4,12},{5,13},{6,14},{7,15},{8,0},{9,1},... | collective-permute-start | bytes 2359304 | tf_op jit(solution)/shard_map/ppermute | solution.py:10
  38.8 40.8 %all-gather.2.cloned.1.call-done = bf16[4096,384]{1,0:T(8,128)(2,1)} async-done(((bf16[256,384]{1,0:T(8,128)(2,1)}), bf16[4096,384]{1,0:T(8,128)(2,1)}) %all-gather.2.cloned.1.call-update) | async-done | bytes 3145744 | tf_op jit(solution)/shard_map/all_gather | solution.py:18
  79.6 0.0 copy-done
  79.6 2.7 %multiply_reduce_fusion.3 = (f32[128]{0:T(128)S(1)}, f32[128,384]{1,0:T(8,128)S(1)}) fusion(bf16[128,4096]{1,0:T(8,128)(2,1)S(1)} %copy-done, bf16[4096,384]{1,0:T(8,128)(2,1)} %all-gather.2.cloned.1.call-done), kind=kOutput, calls=%fused_computation.39 | convolution fusion | flops 402751360 | bytes 4391424 | tf_op jit(solution)/shard_map/dot_general | solution.py:19
  82.3 0.1 multiply_convert_fusion.1
  82.4 0.2 convolution_multiply_fusion.4
  82.6 0.3 fusion.30
  82.9 1.6 collective-permute-done.3
  84.5 1.5 multiply_reduce_fusion
  86.0 0.3 fusion.10
  86.3 1.0 multiply_reduce_fusion.5
  87.2 1.0 multiply_reduce_fusion.4
  88.2 0.3 fusion.27
  88.5 1.2 multiply_reduce_fusion.1
  89.7 0.3 fusion.17
  90.0 0.4 multiply_reduce_fusion.2
  90.4 3.8 %convolution_bitcast_fusion = f32[4096,384]{0,1:T(8,128)} fusion(bf16[128,4096]{1,0:T(8,128)(2,1)S(1)} %copy-done, f32[128,384]{1,0:T(8,128)S(1)} %get-tuple-element.35, f32[128,384]{1,0:T(8,128)S(1)} %get-tuple-element.30, f32[128]{0:T(128)S(1)} %get-tuple-element.34, f32[128]{0:T(128)S(1)} %add_rsqrt_fusion.1), kind=kOutput, calls=%fused_computation | convolution fusion | flops 402898944 | bytes 7734272 | tf_op jit(solution)/shard_map/dot_general | solution.py:92
  94.2 0.0 reduce-scatter.2.cloned.1.call-update
  100.7 33.2 %all-reduce = (f32[1]{0:T(128)}, f32[1]{0:T(128)}) all-reduce(f32[1]{0:T(128)} %bitcast.6, f32[1]{0:T(128)} %bitcast.5), channel_id=1, replica_groups=mesh['group'=2,'dp'=16] {'dp'}, use_global_device_ids=true, to_apply=%region_20.21 | all-reduce | flops 2 | bytes 16 | tf_op jit(solution)/shard_map/psum | solution.py:99
  133.9 1.9 pad_maximum_fusion
  135.7 0.5 negate_subtract_fusion
  136.3 45.5 %reduce-scatter.2.cloned.1.call-done = f32[256,384]{0,1:T(8,128)} async-done(((f32[4096,384]{0,1:T(8,128)}), f32[256,384]{0,1:T(8,128)}) %reduce-scatter.2.cloned.1.call-update) | async-done | bytes 393232 | tf_op jit(solution)/shard_map/reduce_scatter | solution.py:91
  181.7 1.9 %copy.9 = f32[256,384]{1,0:T(8,128)} copy(f32[256,384]{0,1:T(8,128)} %reduce-scatter.2.cloned.1.call-done) | data formatting | bytes 786432
  (7 shorter events, 0.1 us)
Async XLA Ops:
  7.2 72.4 %copy-start = (bf16[128,4096]{1,0:T(8,128)(2,1)S(1)}, bf16[128,4096]{1,0:T(8,128)(2,1)}, u32[]{:S(2)}) copy-start(bf16[128,4096]{1,0:T(8,128)(2,1)} %param.6) | copy-start | bytes 3145732
  7.2 72.4 %all-gather.2.cloned.1.call-start = ((), (), s32[]{:S(2)}) async-start(), calls=%async_computation.1 | async-start | bytes 3342336 | tf_op jit(solution)/shard_map/all_gather | solution.py:18
  7.9 173.8 %reduce-scatter.2.cloned.1.call-start = ((), (), s32[]{:S(2)}) async-start(), calls=%async_computation.2 | async-start | bytes 6684672 | tf_op jit(solution)/shard_map/reduce_scatter | solution.py:91
  10.0 1.6 collective-permute-start
  11.6 7.8 %collective-permute-start.1 = (bf16[256,384]{1,0:T(8,128)(2,1)S(1)}, bf16[256,384]{1,0:T(8,128)(2,1)S(1)}, u32[]{:S(2)}, u32[]{:S(2)}) collective-permute-start(bf16[256,384]{1,0:T(8,128)(2,1)S(1)} %maximum_select_fusion.2), channel_id=1, source_target_pairs={{0,2},{1,3},{2,0},{3,1},{4,6},{5,7},{6,4},{7,5},{8,10},{9,11},{10,... | collective-permute-start | bytes 589832 | tf_op jit(solution)/shard_map/ppermute | solution.py:10
  19.5 16.0 %collective-permute-start.2 = (bf16[512,384]{1,0:T(8,128)(2,1)S(1)}, bf16[512,384]{1,0:T(8,128)(2,1)S(1)}, u32[]{:S(2)}, u32[]{:S(2)}) collective-permute-start(bf16[512,384]{1,0:T(8,128)(2,1)S(1)} %maximum_select_fusion.1), channel_id=1, source_target_pairs={{0,4},{1,5},{2,6},{3,7},{4,0},{5,1},{6,2},{7,3},{8,12},{9,13},{10,... | collective-permute-start | bytes 1179656 | tf_op jit(solution)/shard_map/ppermute | solution.py:10
  35.9 48.6 %collective-permute-start.3 = (bf16[1024,384]{1,0:T(8,128)(2,1)S(1)}, bf16[1024,384]{1,0:T(8,128)(2,1)S(1)}, u32[]{:S(2)}, u32[]{:S(2)}) collective-permute-start(bf16[1024,384]{1,0:T(8,128)(2,1)S(1)} %maximum_select_fusion), channel_id=1, source_target_pairs={{0,8},{1,9},{2,10},{3,11},{4,12},{5,13},{6,14},{7,15},{8,0},{9,1},... | collective-permute-start | bytes 2359304 | tf_op jit(solution)/shard_map/ppermute | solution.py:10
Sparse Core Ops, SparseCore 0:
  10.3 69.2 all-gather.1
  94.3 87.3 reduce-scatter.1
where the time goes:
time: 192 us; the launch traced here: 190 us
  waiting for transfers between devices  108 us (56%)
  blocking collectives  33.2 us (17%)
  between operations  22 us (11%)
  matrix products  12.8 us (7%)
  starting transfers between devices  7.15 us (4%)
  other arithmetic  4.99 us (3%)
  local copies, waits for them, and re-layouts  2.67 us (1%)
    reduce_scatter x1, waiting for transfers between devices, shards(): lax.psum_scatter(lax.dot_general(clips_feat, grad_proj, (((0,), (0,)), ((...  45.5 us
    all_gather x1, waiting for transfers between devices, shards(): full_weight = lax.all_gather(weight, 'dp', axis=0, tiled=True)  40.8 us
    psum x1, blocking collectives, shards(): summed = lax.psum((dscale, dbias), 'dp')  33.2 us
    ppermute x4, waiting for transfers between devices, swapped(): lax.ppermute(x, axis, [(i, i ^ 1 << apart) for i in range(lax.axis_size(a...  20.6 us
    ppermute x4, starting transfers between devices, swapped(): lax.ppermute(x, axis, [(i, i ^ 1 << apart) for i in range(lax.axis_size(a...  7.07 us
    dot_general x5, matrix products, one_tile(): lax.dot_general(clip_unit, block, (((1,), (1,)), ((), ())), preferred_ele...  4.8 us
  transfers between devices with their start and end apart: 6, of which 5 were waited for; matrix products, arithmetic and copies ran while one was open for 5% of the time, Pallas kernels for 0%

commit v1 on v0

--- a/solution.py
+++ b/solution.py
@@ -1,7 +1,252 @@
+import functools
+
 import jax
 import jax.numpy as jnp
 from jax import lax
+from jax.experimental import pallas as pl
+from jax.experimental.pallas import tpu as pltpu
 from jax.sharding import PartitionSpec as P
+
+MESH = pl.DeviceIdType.MESH
+TAIL = 16
+
+
+def fused(n, clips_ref, w_ref, s_ref, ls_ref, bias_ref, pos_ref, loss_ref, gw_ref, sc_ref,
+          wfull, sfull, gfull, cturn, cfull, proj_acc,
+          w_send, w_recv, s_send, s_recv, g_send, g_recv, c_send, c_recv):
+    rows, width = s_ref.shape
+    depth = w_ref.shape[0]
+    group = lax.axis_index("group")
+    me = lax.axis_index("dp")
+    z = me // 4
+    x = (me // 2) % 2
+    c = me % 2
+    mid = (z * (3 - z)) // 2
+    near = z + 1 - 2 * (z % 2)
+    across = 3 - z
+    far = (z + 2) % 4
+    zs = [z, near, mid * across + (1 - mid) * far, mid * far + (1 - mid) * across]
+
+    def at(zz, xx, cc):
+        return zz * 4 + xx * 2 + cc
+
+    barrier = pltpu.get_barrier_semaphore()
+    for k in range(1, n):
+        pl.semaphore_signal(barrier, inc=1, device_id=(group, lax.rem(me + k, n)), device_id_type=MESH)
+
+    wfull[me] = w_ref[...]
+    s32 = s_ref[...].astype(jnp.float32)
+    sfull[me] = (s32 * lax.rsqrt(jnp.sum(s32 * s32, axis=1, keepdims=True) + 1e-06)).astype(jnp.bfloat16)
+    pl.semaphore_wait(barrier, n - 1)
+
+    def block_copy(buf, send, recv, origin, target, k):
+        return pltpu.make_async_remote_copy(
+            src_ref=buf.at[origin], dst_ref=buf.at[origin], send_sem=send.at[k],
+            recv_sem=recv.at[origin], device_id=(group, target), device_id_type=MESH)
+
+    z_out = at(near, x, c)
+    z_mid = at(across, x, c)
+    x_out = at(z, 1 - x, c)
+    c_out = at(z, x, 1 - c)
+    W = (wfull, w_send, w_recv)
+    S = (sfull, s_send, s_recv)
+    G = (gfull, g_send, g_recv)
+
+    def z_step(array, i):
+        buf, send, recv = array
+        origin = at(zs[i], x, c)
+        if i > 0:
+            block_copy(buf, send, recv, origin, me + 1 - 2 * c, 0).wait_recv()
+        if i == 0:
+            block_copy(buf, send, recv, origin, z_out, 0).start()
+        if i < 2:
+            @pl.when(mid == 1)
+            def _():
+                block_copy(buf, send, recv, origin, z_mid, 1 + i).start()
+        else:
+            @pl.when(mid == 1)
+            def _():
+                block_copy(buf, send, recv, origin, z_out, 1 + i).start()
+        block_copy(buf, send, recv, origin, x_out, 5 + i).start()
+        block_copy(buf, send, recv, origin, c_out, 9 + i).start()
+        return origin
+
+    def x_step(array, i):
+        buf, send, recv = array
+        origin = at(zs[i], 1 - x, c)
+        block_copy(buf, send, recv, origin, c_out, 0).wait_recv()
+        block_copy(buf, send, recv, origin, c_out, 13 + i).start()
+        return origin
+
+    def c_step(array, i, xx):
+        buf, send, recv = array
+        origin = at(zs[i], xx, 1 - c)
+        block_copy(buf, send, recv, origin, c_out, 0).wait_recv()
+        return origin
+
+    def drain(array):
+        buf, send, recv = array
+        for k in range(17):
+            if 1 <= k <= 4:
+                @pl.when(mid == 1)
+                def _():
+                    block_copy(buf, send, recv, me, c_out, k).wait_send()
+            else:
+                block_copy(buf, send, recv, me, c_out, k).wait_send()
+
+    proj_acc[...] = jnp.zeros_like(proj_acc)
+
+    def project(origin):
+        columns = pl.ds(pl.multiple_of(origin * depth, depth), depth)
+        proj_acc[...] += jnp.dot(clips_ref[:, columns], wfull[origin], preferred_element_type=jnp.float32)
+
+    def turn_copy(k):
+        target = lax.rem(me + k, n)
+        mine = pl.ds(pl.multiple_of(me * rows, rows), rows)
+        return pltpu.make_async_remote_copy(
+            src_ref=cturn.at[target], dst_ref=cfull.at[:, mine], send_sem=c_send.at[k],
+            recv_sem=c_recv.at[k], device_id=(group, target), device_id_type=MESH)
+
+    def turn(k):
+        target = lax.rem(me + k, n)
+        columns = pl.ds(pl.multiple_of(target * depth, depth), depth)
+        block = clips_ref[:, columns].T
+        if k == 0:
+            cfull[:, pl.ds(pl.multiple_of(me * rows, rows), rows)] = block
+        else:
+            cturn[target] = block
+
+    z_step(W, 0)
+    z_step(S, 0)
+    project(me)
+    for k in range(n):
+        turn(k)
+    for i in range(1, 4):
+        origin = z_step(W, i)
+        z_step(S, i)
+        project(origin)
+    for k in range(1, n):
+        turn_copy(k).start()
+    for i in range(4):
+        origin = x_step(W, i)
+        x_step(S, i)
+        project(origin)
+    for i in range(4):
+        project(c_step(W, i, x))
+        c_step(S, i, x)
+    for i in range(4):
+        project(c_step(W, i, 1 - x))
+        c_step(S, i, 1 - x)
+
+    proj = proj_acc[...]
+    inverse = lax.rsqrt(jnp.sum(proj * proj, axis=1, keepdims=True) + 1e-06)
+    unit32 = proj * inverse
+    clip_unit = unit32.astype(jnp.bfloat16)
+    span = 4 * rows
+    scale = jnp.exp(jnp.full((1, span), ls_ref[0], jnp.float32))
+    shift = bias_ref[0]
+    inv_count = 1.0 / (rows * n)
+    first_pos = pos_ref[:, 0:1]
+    second_pos = pos_ref[:, 1:2]
+    grad = jnp.zeros((rows, width), jnp.float32)
+    losses = jnp.zeros((rows, 1), jnp.float32)
+    dscale = jnp.zeros((1, span), jnp.float32)
+    dbias = jnp.zeros((1, span), jnp.float32)
+    for i in range(n // 4):
+        block = sfull[4 * i:4 * i + 4].reshape(span, width)
+        products = lax.dot_general(clip_unit, block, (((1,), (1,)), ((), ())), preferred_element_type=jnp.float32)
+        scaled = scale * products
+        logits = scaled + shift
+        columns = i * span + lax.broadcasted_iota(jnp.int32, (rows, span), 1)
+        matched = (first_pos == columns) | (second_pos == columns)
+        margin = jnp.where(matched, logits, -logits)
+        small = jnp.exp(-jnp.abs(margin))
+        losses = losses + jnp.sum(jnp.maximum(-margin, 0.0) + jnp.log1p(small), axis=1, keepdims=True)
+        chance = jnp.where(margin >= 0.0, small, 1.0) / (1.0 + small) * inv_count
+        grad_logit = jnp.where(matched, -chance, chance)
+        dscale = dscale + jnp.sum(grad_logit * scaled, axis=0, keepdims=True)
+        dbias = dbias + jnp.sum(grad_logit, axis=0, keepdims=True)
+        grad = grad + jnp.dot(grad_logit.astype(jnp.bfloat16), block, preferred_element_type=jnp.float32)
+    grad_unit = scale[:, :width] * grad
+    inner = jnp.sum(unit32 * grad_unit, axis=1, keepdims=True)
+    gfull[me, :rows, :] = (inverse * (grad_unit - unit32 * inner)).astype(jnp.bfloat16)
+    both = jnp.where(lax.broadcasted_iota(jnp.int32, (TAIL, width), 1) < 128,
+                     jnp.sum(dscale, axis=1, keepdims=True), jnp.sum(dbias, axis=1, keepdims=True))
+    high = both.astype(jnp.bfloat16)
+    rest = both - high.astype(jnp.float32)
+    middle = rest.astype(jnp.bfloat16)
+    low = rest - middle.astype(jnp.float32)
+    row = lax.broadcasted_iota(jnp.int32, (TAIL, width), 0)
+    pieces = jnp.where(row == 0, high.astype(jnp.float32),
+                       jnp.where(row == 1, middle.astype(jnp.float32), jnp.where(row == 2, low, 0.0)))
+    gfull[me, rows:, :] = pieces.astype(jnp.bfloat16)
+
+    z_step(G, 0)
+    square = lax.broadcasted_iota(jnp.int32, (rows, rows), 0) == lax.broadcasted_iota(jnp.int32, (rows, rows), 1)
+    loss_ref[...] = jnp.sum(jnp.where(square, losses, 0.0), axis=0, keepdims=True)
+    for k in range(1, n):
+        turn_copy(k).wait_recv()
+
+    def weigh(origin, first=False):
+        columns = pl.ds(pl.multiple_of(origin * rows, rows), rows)
+        term = jnp.dot(cfull[:, columns], gfull[origin, :rows, :], preferred_element_type=jnp.float32)
+        if first:
+            gw_ref[...] = term
+        else:
+            gw_ref[...] += term
+
+    weigh(me, True)
+    for i in range(1, 4):
+        weigh(z_step(G, i))
+    for i in range(4):
+        weigh(x_step(G, i))
+    for i in range(4):
+        weigh(c_step(G, i, x))
+    for i in range(4):
+        weigh(c_step(G, i, 1 - x))
+    tails = jnp.zeros((TAIL, width), jnp.float32)
+    for p in range(n):
+        tails = tails + gfull[p, rows:, :].astype(jnp.float32)
+    sc_ref[0] = jnp.sum(tails[:, 0:1])
+    sc_ref[1] = jnp.sum(tails[:, 128:129])
+    drain(W)
+    drain(S)
+    drain(G)
+    for k in range(1, n):
+        turn_copy(k).wait_send()
+
+
+def in_kernel(clips_feat, weight, sentences, log_scale, bias, positives):
+    n = lax.axis_size("dp")
+    rows, features = clips_feat.shape
+    depth, width = weight.shape
+    vmem = pl.BlockSpec(memory_space=pltpu.VMEM)
+    smem = pl.BlockSpec(memory_space=pltpu.SMEM)
+    dma = pltpu.SemaphoreType.DMA
+    loss, grad_weight, scalars = pl.pallas_call(
+        functools.partial(fused, n),
+        out_shape=(
+            jax.ShapeDtypeStruct((1, rows), jnp.float32),
+            jax.ShapeDtypeStruct((depth, width), jnp.float32),
+            jax.ShapeDtypeStruct((2,), jnp.float32),
+        ),
+        in_specs=[vmem, vmem, vmem, smem, smem, vmem],
+        out_specs=(vmem, vmem, smem),
+        scratch_shapes=[
+            pltpu.VMEM((n, depth, width), jnp.bfloat16),
+            pltpu.VMEM((n, rows, width), jnp.bfloat16),
+            pltpu.VMEM((n, rows + TAIL, width), jnp.bfloat16),
+            pltpu.VMEM((n, depth, rows), jnp.bfloat16),
+            pltpu.VMEM((depth, n * rows), jnp.bfloat16),
+            pltpu.VMEM((rows, width), jnp.float32),
+            dma((17,)), dma((n,)), dma((17,)), dma((n,)), dma((17,)), dma((n,)), dma((n,)), dma((n,)),
+        ],
+        compiler_params=pltpu.CompilerParams(
+            collective_id=0, has_side_effects=True, vmem_limit_bytes=40 * 1024 * 1024),
+        cost_estimate=pl.CostEstimate(flops=1300000000, bytes_accessed=3000000, transcendentals=1000000),
+    )(clips_feat, weight, sentences, log_scale, bias, positives)
+    return loss.reshape(rows), grad_weight, scalars
+
 
 column_block = 2048
 
@@ -111,4 +356,5 @@
         P(("group", "dp"), None),
     )
     out_specs = (P(("group", "dp")), P(("group", "dp"), None), P("group"))
-    return jax.shard_map(shards, mesh=mesh, in_specs=in_specs, out_specs=out_specs, check_vma=False)
+    body = in_kernel if mesh.shape["dp"] == 16 else shards
+    return jax.shard_map(body, mesh=mesh, in_specs=in_specs, out_specs=out_specs, check_vma=False)

time: 192 us -> 76.5 us (0.40)
  waiting for transfers between devices: 108 us -> 0 us
  Pallas kernels: 0 us -> 69.4 us
  blocking collectives: 33.2 us -> 0 us
  between operations: 22 us -> 1.96 us
  matrix products: 12.8 us -> 0 us
  starting transfers between devices: 7.15 us -> 0 us
  other arithmetic: 4.99 us -> 0 us
  local copies, waits for them, and re-layouts: 2.67 us -> 4.93 us
    pallas_call x0 -> x1, Pallas kernels: none -> 69.4 us  [in_kernel(): pl.pallas_call(functools.partial(fused, n), out_shape=(jax.ShapeDtypeStru...]
    reduce_scatter x1 -> x0, waiting for transfers between devices: 45.5 us -> none  [shards(): lax.psum_scatter(lax.dot_general(clips_feat, grad_proj, (((0,), (0,)), ((...]
    all_gather x1 -> x0, waiting for transfers between devices: 40.8 us -> none  [shards(): full_weight = lax.all_gather(weight, 'dp', axis=0, tiled=True)]
    psum x1 -> x0, blocking collectives: 33.2 us -> none  [shards(): summed = lax.psum((dscale, dbias), 'dp')]
    ppermute x4 -> x0, waiting for transfers between devices: 20.6 us -> none  [swapped(): lax.ppermute(x, axis, [(i, i ^ 1 << apart) for i in range(lax.axis_size(a...]
    dot_general x12 -> x0, matrix products: 12.8 us -> none  [the longest x5 4.8 us: one_tile(): lax.dot_general(clip_unit, block, (((1,), (1,)), ((), ())), preferred_ele...]
    ppermute x4 -> x0, starting transfers between devices: 7.07 us -> none  [swapped(): lax.ppermute(x, axis, [(i, i ^ 1 << apart) for i in range(lax.axis_size(a...]
    unnamed x3 -> x12, local copies, waits for them, and re-layouts: 1.92 us -> 4.93 us
  transfers between devices with their start and end apart: 6 -> 0, of which waited for: 5 -> 0; matrix products, arithmetic and copies ran while one was open for 5% -> 0% of each run, Pallas kernels for 0% -> 0%
where the time goes in v1:
time: 76.5 us; the launch traced here: 76.3 us
  Pallas kernels  69.4 us (91%)
  local copies, waits for them, and re-layouts  4.93 us (6%)
  between operations  1.96 us (3%)
    pallas_call x1, Pallas kernels, in_kernel(): pl.pallas_call(functools.partial(fused, n), out_shape=(jax.ShapeDtypeStru...  69.4 us
    unnamed x12, local copies, waits for them, and re-layouts  4.93 us

profile of v1, /device:TPU:1, one launch (start us, length us, event | category | flops | bytes accessed | tf_op | source)
XLA Modules:
  0.0 76.3 jit_solution(9357493391672604436)
XLA Ops:
  1.3 0.0 copy-start.3
  1.9 0.0 copy-done.3
  2.0 0.1 copy.9.pos_ref
  2.1 0.0 copy-start
  2.1 1.2 %copy-done = bf16[128,4096]{1,0:T(8,128)(2,1)S(1)} copy-done((bf16[128,4096]{1,0:T(8,128)(2,1)S(1)}, bf16[128,4096]{1,0:T(8,128)(2,1)}, u32[]{:S(2)}) %copy-start) | copy-done | bytes 1048600
  3.3 0.0 copy-start.1
  3.3 0.9 %copy-done.1 = bf16[256,384]{1,0:T(8,128)(2,1)S(1)} copy-done((bf16[256,384]{1,0:T(8,128)(2,1)S(1)}, bf16[256,384]{1,0:T(8,128)(2,1)}, u32[]{:S(2)}) %copy-start.1) | copy-done | bytes 196632
  4.2 0.0 copy-start.2
  4.2 0.9 %copy-done.2 = bf16[128,384]{1,0:T(8,128)(2,1)S(1)} copy-done((bf16[128,384]{1,0:T(8,128)(2,1)S(1)}, bf16[128,384]{1,0:T(8,128)(2,1)}, u32[]{:S(2)}) %copy-start.2) | copy-done | bytes 98328
  5.1 69.4 %shard_map.85 = (f32[1,128]{1,0:T(1,128)S(1)}, f32[256,384]{1,0:T(8,128)S(1)}, f32[2]{0:T(128)S(1)}) custom-call(bf16[128,4096]{1,0:T(8,128)(2,1)S(1)} %copy-done, bf16[256,384]{1,0:T(8,128)(2,1)S(1)} %copy-done.1, bf16[128,384]{1,0:T(8,128)(2,1)S(1)} %copy-done.2, f32[1]{0:T(128)S(6)} %copy.13.ls_ref, f32[1]{0:T(128)S(6)} %copy.14.bias_ref, ...), custom_call_target="tpu_custom_call" | custom-call | flops 1300000000 | bytes 3000000 | tf_op jit(solution)/shard_map/pallas_call | solution.py:226
  74.5 0.5 copy.15
  75.0 0.7 copy.16
  75.8 0.5 copy.17
Async XLA Ops:
  1.3 0.7 copy-start.3
  2.1 1.2 %copy-start = (bf16[128,4096]{1,0:T(8,128)(2,1)S(1)}, bf16[128,4096]{1,0:T(8,128)(2,1)}, u32[]{:S(2)}) copy-start(bf16[128,4096]{1,0:T(8,128)(2,1)} %clips_ref.1) | copy-start | bytes 3145732
  3.3 0.9 %copy-start.1 = (bf16[256,384]{1,0:T(8,128)(2,1)S(1)}, bf16[256,384]{1,0:T(8,128)(2,1)}, u32[]{:S(2)}) copy-start(bf16[256,384]{1,0:T(8,128)(2,1)} %w_ref.1) | copy-start | bytes 589828
  4.2 0.9 %copy-start.2 = (bf16[128,384]{1,0:T(8,128)(2,1)S(1)}, bf16[128,384]{1,0:T(8,128)(2,1)}, u32[]{:S(2)}) copy-start(bf16[128,384]{1,0:T(8,128)(2,1)} %s_ref.1) | copy-start | bytes 294916

commit v2 on v1

--- a/solution.py
+++ b/solution.py
@@ -11,11 +11,11 @@
 TAIL = 16
 
 
-def fused(n, clips_ref, w_ref, s_ref, ls_ref, bias_ref, pos_ref, loss_ref, gw_ref, sc_ref,
-          wfull, sfull, gfull, cturn, cfull, proj_acc,
+def fused(n, clips_hbm, w_hbm, s_hbm, ls_ref, bias_ref, pos_ref, loss_ref, gw_ref, sc_ref,
+          clips_ref, s_ref, wfull, sfull, gfull, cturn, cfull, proj_acc, in_sem,
           w_send, w_recv, s_send, s_recv, g_send, g_recv, c_send, c_recv):
     rows, width = s_ref.shape
-    depth = w_ref.shape[0]
+    depth = w_hbm.shape[0]
     group = lax.axis_index("group")
     me = lax.axis_index("dp")
     z = me // 4
@@ -30,19 +30,30 @@
     def at(zz, xx, cc):
         return zz * 4 + xx * 2 + cc
 
+    w_in = pltpu.make_async_copy(w_hbm, wfull.at[me], in_sem.at[0])
+    s_in = pltpu.make_async_copy(s_hbm, s_ref, in_sem.at[1])
+    clips_in = pltpu.make_async_copy(clips_hbm, clips_ref, in_sem.at[2])
+    w_in.start()
+    s_in.start()
+    clips_in.start()
     barrier = pltpu.get_barrier_semaphore()
     for k in range(1, n):
         pl.semaphore_signal(barrier, inc=1, device_id=(group, lax.rem(me + k, n)), device_id_type=MESH)
 
-    wfull[me] = w_ref[...]
+    s_in.wait()
     s32 = s_ref[...].astype(jnp.float32)
-    sfull[me] = (s32 * lax.rsqrt(jnp.sum(s32 * s32, axis=1, keepdims=True) + 1e-06)).astype(jnp.bfloat16)
+    sfull[(x * 2 + c) * 4 + z] = (s32 * lax.rsqrt(jnp.sum(s32 * s32, axis=1, keepdims=True) + 1e-06)).astype(jnp.bfloat16)
+    w_in.wait()
     pl.semaphore_wait(barrier, n - 1)
 
     def block_copy(buf, send, recv, origin, target, k):
+        slot = sent_slot(origin) if buf is sfull else origin
         return pltpu.make_async_remote_copy(
-            src_ref=buf.at[origin], dst_ref=buf.at[origin], send_sem=send.at[k],
+            src_ref=buf.at[slot], dst_ref=buf.at[slot], send_sem=send.at[k],
             recv_sem=recv.at[origin], device_id=(group, target), device_id_type=MESH)
+
+    def sent_slot(origin):
+        return (origin % 4) * 4 + origin // 4
 
     z_out = at(near, x, c)
     z_mid = at(across, x, c)
@@ -100,43 +111,66 @@
         columns = pl.ds(pl.multiple_of(origin * depth, depth), depth)
         proj_acc[...] += jnp.dot(clips_ref[:, columns], wfull[origin], preferred_element_type=jnp.float32)
 
+    def turn_target(k):
+        return at((z + k // 4) % 4, (x + (k // 2) % 2) % 2, (c + k % 2) % 2)
+
     def turn_copy(k):
-        target = lax.rem(me + k, n)
         mine = pl.ds(pl.multiple_of(me * rows, rows), rows)
         return pltpu.make_async_remote_copy(
-            src_ref=cturn.at[target], dst_ref=cfull.at[:, mine], send_sem=c_send.at[k],
-            recv_sem=c_recv.at[k], device_id=(group, target), device_id_type=MESH)
+            src_ref=cturn.at[k], dst_ref=cfull.at[:, mine], send_sem=c_send.at[k],
+            recv_sem=c_recv.at[k], device_id=(group, turn_target(k)), device_id_type=MESH)
 
     def turn(k):
-        target = lax.rem(me + k, n)
-        columns = pl.ds(pl.multiple_of(target * depth, depth), depth)
+        columns = pl.ds(pl.multiple_of(turn_target(k) * depth, depth), depth)
         block = clips_ref[:, columns].T
         if k == 0:
             cfull[:, pl.ds(pl.multiple_of(me * rows, rows), rows)] = block
         else:
-            cturn[target] = block
+            cturn[k] = block
+            turn_copy(k).start()
 
     z_step(W, 0)
     z_step(S, 0)
+    clips_in.wait()
     project(me)
-    for k in range(n):
-        turn(k)
-    for i in range(1, 4):
-        origin = z_step(W, i)
-        z_step(S, i)
-        project(origin)
-    for k in range(1, n):
-        turn_copy(k).start()
-    for i in range(4):
-        origin = x_step(W, i)
-        x_step(S, i)
-        project(origin)
-    for i in range(4):
-        project(c_step(W, i, x))
-        c_step(S, i, x)
-    for i in range(4):
-        project(c_step(W, i, 1 - x))
-        c_step(S, i, 1 - x)
+    turn(0)
+    project(z_step(W, 1))
+    z_step(S, 1)
+    project(z_step(W, 2))
+    z_step(S, 2)
+    project(z_step(W, 3))
+    z_step(S, 3)
+    turn(9)
+    turn(12)
+    turn(5)
+    turn(8)
+    turn(4)
+    turn(13)
+    turn(1)
+    project(x_step(W, 0))
+    x_step(S, 0)
+    project(x_step(W, 1))
+    x_step(S, 1)
+    project(x_step(W, 2))
+    x_step(S, 2)
+    project(x_step(W, 3))
+    x_step(S, 3)
+    turn(10)
+    turn(11)
+    turn(6)
+    turn(7)
+    turn(14)
+    turn(15)
+    turn(2)
+    turn(3)
+    project(c_step(W, 0, x))
+    project(c_step(W, 1, x))
+    project(c_step(W, 2, x))
+    project(c_step(W, 3, x))
+    project(c_step(W, 0, 1 - x))
+    project(c_step(W, 1, 1 - x))
+    project(c_step(W, 2, 1 - x))
+    project(c_step(W, 3, 1 - x))
 
     proj = proj_acc[...]
     inverse = lax.rsqrt(jnp.sum(proj * proj, axis=1, keepdims=True) + 1e-06)
@@ -152,12 +186,17 @@
     losses = jnp.zeros((rows, 1), jnp.float32)
     dscale = jnp.zeros((1, span), jnp.float32)
     dbias = jnp.zeros((1, span), jnp.float32)
-    for i in range(n // 4):
-        block = sfull[4 * i:4 * i + 4].reshape(span, width)
+    for xx, cc in ((x, c), (1 - x, c), (x, 1 - c), (1 - x, 1 - c)):
+        if cc is not c:
+            for i in range(4):
+                c_step(S, i, xx)
+        place = xx * 2 + cc
+        block = sfull[pl.ds(place * 4, 4)].reshape(span, width)
         products = lax.dot_general(clip_unit, block, (((1,), (1,)), ((), ())), preferred_element_type=jnp.float32)
         scaled = scale * products
         logits = scaled + shift
-        columns = i * span + lax.broadcasted_iota(jnp.int32, (rows, span), 1)
+        lane = lax.broadcasted_iota(jnp.int32, (1, span), 1)
+        columns = (lane // rows * 4 + place) * rows + lane % rows
         matched = (first_pos == columns) | (second_pos == columns)
         margin = jnp.where(matched, logits, -logits)
         small = jnp.exp(-jnp.abs(margin))
@@ -221,6 +260,7 @@
     rows, features = clips_feat.shape
     depth, width = weight.shape
     vmem = pl.BlockSpec(memory_space=pltpu.VMEM)
+    hbm = pl.BlockSpec(memory_space=pl.ANY)
     smem = pl.BlockSpec(memory_space=pltpu.SMEM)
     dma = pltpu.SemaphoreType.DMA
     loss, grad_weight, scalars = pl.pallas_call(
@@ -230,16 +270,18 @@
             jax.ShapeDtypeStruct((depth, width), jnp.float32),
             jax.ShapeDtypeStruct((2,), jnp.float32),
         ),
-        in_specs=[vmem, vmem, vmem, smem, smem, vmem],
+        in_specs=[hbm, hbm, hbm, smem, smem, vmem],
         out_specs=(vmem, vmem, smem),
         scratch_shapes=[
+            pltpu.VMEM((rows, features), jnp.bfloat16),
+            pltpu.VMEM((rows, width), jnp.bfloat16),
             pltpu.VMEM((n, depth, width), jnp.bfloat16),
             pltpu.VMEM((n, rows, width), jnp.bfloat16),
             pltpu.VMEM((n, rows + TAIL, width), jnp.bfloat16),
             pltpu.VMEM((n, depth, rows), jnp.bfloat16),
             pltpu.VMEM((depth, n * rows), jnp.bfloat16),
             pltpu.VMEM((rows, width), jnp.float32),
-            dma((17,)), dma((n,)), dma((17,)), dma((n,)), dma((17,)), dma((n,)), dma((n,)), dma((n,)),
+            dma((3,)), dma((17,)), dma((n,)), dma((17,)), dma((n,)), dma((17,)), dma((n,)), dma((n,)), dma((n,)),
         ],
         compiler_params=pltpu.CompilerParams(
             collective_id=0, has_side_effects=True, vmem_limit_bytes=40 * 1024 * 1024),

time: 76.5 us -> 72.7 us (0.950)
  Pallas kernels: 69.4 us -> 65.6 us
    pallas_call x1, Pallas kernels: 69.4 us -> 65.6 us  [in_kernel(): pl.pallas_call(functools.partial(fused, n), out_shape=(jax.ShapeDtypeStru...]
where the time goes in v2:
time: 72.7 us; the launch traced here: 72.5 us
  Pallas kernels  65.6 us (90%)
  local copies, waits for them, and re-layouts  4.93 us (7%)
  between operations  1.96 us (3%)
    pallas_call x1, Pallas kernels, in_kernel(): pl.pallas_call(functools.partial(fused, n), out_shape=(jax.ShapeDtypeStru...  65.6 us
    unnamed x12, local copies, waits for them, and re-layouts  4.93 us

profile of v2, /device:TPU:1, one launch (start us, length us, event | category | flops | bytes accessed | tf_op | source)
XLA Modules:
  0.0 72.5 jit_solution(13863999839711774806)
XLA Ops:
  1.3 0.0 copy-start.3
  1.9 0.0 copy-done.3
  2.0 0.1 copy.9.pos_ref
  2.1 0.0 copy-start
  2.1 1.2 %copy-done = bf16[128,4096]{1,0:T(8,128)(2,1)S(1)} copy-done((bf16[128,4096]{1,0:T(8,128)(2,1)S(1)}, bf16[128,4096]{1,0:T(8,128)(2,1)}, u32[]{:S(2)}) %copy-start) | copy-done | bytes 1048600
  3.3 0.0 copy-start.1
  3.3 0.9 %copy-done.1 = bf16[256,384]{1,0:T(8,128)(2,1)S(1)} copy-done((bf16[256,384]{1,0:T(8,128)(2,1)S(1)}, bf16[256,384]{1,0:T(8,128)(2,1)}, u32[]{:S(2)}) %copy-start.1) | copy-done | bytes 196632
  4.2 0.0 copy-start.2
  4.2 0.9 %copy-done.2 = bf16[128,384]{1,0:T(8,128)(2,1)S(1)} copy-done((bf16[128,384]{1,0:T(8,128)(2,1)S(1)}, bf16[128,384]{1,0:T(8,128)(2,1)}, u32[]{:S(2)}) %copy-start.2) | copy-done | bytes 98328
  5.1 65.6 %shard_map.85 = (f32[1,128]{1,0:T(1,128)S(1)}, f32[256,384]{1,0:T(8,128)S(1)}, f32[2]{0:T(128)S(1)}) custom-call(bf16[128,4096]{1,0:T(8,128)(2,1)S(1)} %copy-done, bf16[256,384]{1,0:T(8,128)(2,1)S(1)} %copy-done.1, bf16[128,384]{1,0:T(8,128)(2,1)S(1)} %copy-done.2, f32[1]{0:T(128)S(6)} %copy.13.ls_ref, f32[1]{0:T(128)S(6)} %copy.14.bias_ref, ...), custom_call_target="tpu_custom_call" | custom-call | flops 1300000000 | bytes 3000000 | tf_op jit(solution)/shard_map/pallas_call | solution.py:266
  70.7 0.5 copy.15
  71.2 0.7 %copy.16 = f32[256,384]{1,0:T(8,128)} copy(f32[256,384]{1,0:T(8,128)S(1)} %get-tuple-element.13) | data formatting | bytes 786432
  72.0 0.5 copy.17
Async XLA Ops:
  1.3 0.7 copy-start.3
  2.1 1.2 %copy-start = (bf16[128,4096]{1,0:T(8,128)(2,1)S(1)}, bf16[128,4096]{1,0:T(8,128)(2,1)}, u32[]{:S(2)}) copy-start(bf16[128,4096]{1,0:T(8,128)(2,1)} %clips_hbm.1) | copy-start | bytes 3145732
  3.3 0.9 %copy-start.1 = (bf16[256,384]{1,0:T(8,128)(2,1)S(1)}, bf16[256,384]{1,0:T(8,128)(2,1)}, u32[]{:S(2)}) copy-start(bf16[256,384]{1,0:T(8,128)(2,1)} %w_hbm.1) | copy-start | bytes 589828
  4.2 0.9 %copy-start.2 = (bf16[128,384]{1,0:T(8,128)(2,1)S(1)}, bf16[128,384]{1,0:T(8,128)(2,1)}, u32[]{:S(2)}) copy-start(bf16[128,384]{1,0:T(8,128)(2,1)} %s_hbm.1) | copy-start | bytes 294916

commit v3 on v2

--- a/solution.py
+++ b/solution.py
@@ -13,7 +13,7 @@
 
 def fused(n, clips_hbm, w_hbm, s_hbm, ls_ref, bias_ref, pos_ref, loss_ref, gw_ref, sc_ref,
           clips_ref, s_ref, wfull, sfull, gfull, cturn, cfull, proj_acc, in_sem,
-          w_send, w_recv, s_send, s_recv, g_send, g_recv, c_send, c_recv):
+          w_send, w_recv, s_send, s_recv, g_send, g_recv, c_send, c_recv, y_send, y_recv):
     rows, width = s_ref.shape
     depth = w_hbm.shape[0]
     group = lax.axis_index("group")
@@ -39,12 +39,13 @@
     barrier = pltpu.get_barrier_semaphore()
     for k in range(1, n):
         pl.semaphore_signal(barrier, inc=1, device_id=(group, lax.rem(me + k, n)), device_id_type=MESH)
+    pl.semaphore_signal(barrier, inc=1, device_id=(1 - group, me), device_id_type=MESH)
 
     s_in.wait()
     s32 = s_ref[...].astype(jnp.float32)
     sfull[(x * 2 + c) * 4 + z] = (s32 * lax.rsqrt(jnp.sum(s32 * s32, axis=1, keepdims=True) + 1e-06)).astype(jnp.bfloat16)
     w_in.wait()
-    pl.semaphore_wait(barrier, n - 1)
+    pl.semaphore_wait(barrier, n)
 
     def block_copy(buf, send, recv, origin, target, k):
         slot = sent_slot(origin) if buf is sfull else origin
@@ -62,6 +63,59 @@
     W = (wfull, w_send, w_recv)
     S = (sfull, s_send, s_recv)
     G = (gfull, g_send, g_recv)
+
+    half = depth // 2
+
+    def half_copy(origin, target, k):
+        part = wfull.at[origin, pl.ds(pl.multiple_of(group * half, half), half), :]
+        return pltpu.make_async_remote_copy(
+            src_ref=part, dst_ref=part, send_sem=w_send.at[k],
+            recv_sem=w_recv.at[origin], device_id=(group, target), device_id_type=MESH)
+
+    def twin_copy(i, which):
+        origin = at(zs[i + 1], x, c) if i < 3 else at(zs[i - 3], 1 - x, c)
+        part = wfull.at[origin, pl.ds(pl.multiple_of(which * half, half), half), :]
+        return pltpu.make_async_remote_copy(
+            src_ref=part, dst_ref=part, send_sem=y_send.at[i],
+            recv_sem=y_recv.at[i], device_id=(1 - group, me), device_id_type=MESH)
+
+    def wz_step(i):
+        origin = at(zs[i], x, c)
+        if i > 0:
+            half_copy(origin, z_out, 0).wait_recv()
+        if i == 0:
+            half_copy(origin, z_out, 0).start()
+        @pl.when(mid == 1)
+        def _():
+            half_copy(origin, z_mid if i < 2 else z_out, 1 + i).start()
+        half_copy(origin, x_out, 5 + i).start()
+        if i == 0:
+            block_copy(wfull, w_send, w_recv, origin, c_out, 9).start()
+        else:
+            twin_copy(i - 1, group).start()
+
+    def wx_step(i):
+        half_copy(at(zs[i], 1 - x, c), x_out, 0).wait_recv()
+        twin_copy(i + 3, group).start()
+
+    def twin_step(i):
+        origin = at(zs[i + 1], x, c) if i < 3 else at(zs[i - 3], 1 - x, c)
+        twin_copy(i, 1 - group).wait_recv()
+        block_copy(wfull, w_send, w_recv, origin, c_out, 10 + i).start()
+        return origin
+
+    def drain_halves():
+        for k in range(9):
+            if 1 <= k <= 4:
+                @pl.when(mid == 1)
+                def _():
+                    half_copy(me, c_out, k).wait_send()
+            else:
+                half_copy(me, c_out, k).wait_send()
+        for k in range(9, 17):
+            block_copy(wfull, w_send, w_recv, me, c_out, k).wait_send()
+        for i in range(7):
+            twin_copy(i, group).wait_send()
 
     def z_step(array, i):
         buf, send, recv = array
@@ -129,16 +183,16 @@
             cturn[k] = block
             turn_copy(k).start()
 
-    z_step(W, 0)
+    wz_step(0)
     z_step(S, 0)
     clips_in.wait()
     project(me)
     turn(0)
-    project(z_step(W, 1))
+    wz_step(1)
     z_step(S, 1)
-    project(z_step(W, 2))
+    wz_step(2)
     z_step(S, 2)
-    project(z_step(W, 3))
+    wz_step(3)
     z_step(S, 3)
     turn(9)
     turn(12)
@@ -147,13 +201,16 @@
     turn(4)
     turn(13)
     turn(1)
-    project(x_step(W, 0))
+    wx_step(0)
     x_step(S, 0)
-    project(x_step(W, 1))
+    project(twin_step(0))
+    wx_step(1)
     x_step(S, 1)
-    project(x_step(W, 2))
+    project(twin_step(1))
+    wx_step(2)
     x_step(S, 2)
-    project(x_step(W, 3))
+    project(twin_step(2))
+    wx_step(3)
     x_step(S, 3)
     turn(10)
     turn(11)
@@ -163,6 +220,10 @@
     turn(15)
     turn(2)
     turn(3)
+    project(twin_step(3))
+    project(twin_step(4))
+    project(twin_step(5))
+    project(twin_step(6))
     project(c_step(W, 0, x))
     project(c_step(W, 1, x))
     project(c_step(W, 2, x))
@@ -248,7 +309,7 @@
         tails = tails + gfull[p, rows:, :].astype(jnp.float32)
     sc_ref[0] = jnp.sum(tails[:, 0:1])
     sc_ref[1] = jnp.sum(tails[:, 128:129])
-    drain(W)
+    drain_halves()
     drain(S)
     drain(G)
     for k in range(1, n):
@@ -282,6 +343,7 @@
             pltpu.VMEM((depth, n * rows), jnp.bfloat16),
             pltpu.VMEM((rows, width), jnp.float32),
             dma((3,)), dma((17,)), dma((n,)), dma((17,)), dma((n,)), dma((17,)), dma((n,)), dma((n,)), dma((n,)),
+            dma((7,)), dma((7,)),
         ],
         compiler_params=pltpu.CompilerParams(
             collective_id=0, has_side_effects=True, vmem_limit_bytes=40 * 1024 * 1024),
@@ -398,5 +460,5 @@
         P(("group", "dp"), None),
     )
     out_specs = (P(("group", "dp")), P(("group", "dp"), None), P("group"))
-    body = in_kernel if mesh.shape["dp"] == 16 else shards
+    body = in_kernel if mesh.shape["dp"] == 16 and mesh.shape["group"] == 2 else shards
     return jax.shard_map(body, mesh=mesh, in_specs=in_specs, out_specs=out_specs, check_vma=False)

time: 72.7 us -> 66.2 us (0.911)
  Pallas kernels: 65.6 us -> 59 us
    pallas_call x1, Pallas kernels: 65.6 us -> 59 us  [in_kernel(): pl.pallas_call(functools.partial(fused, n), out_shape=(jax.ShapeDtypeStru...]
where the time goes in v3:
time: 66.2 us; the launch traced here: 65.9 us
  Pallas kernels  59 us (89%)
  local copies, waits for them, and re-layouts  4.93 us (7%)
  between operations  1.96 us (3%)
    pallas_call x1, Pallas kernels, in_kernel(): pl.pallas_call(functools.partial(fused, n), out_shape=(jax.ShapeDtypeStru...  59 us
    unnamed x12, local copies, waits for them, and re-layouts  4.93 us

profile of v3, /device:TPU:1, one launch (start us, length us, event | category | flops | bytes accessed | tf_op | source)
XLA Modules:
  0.0 65.9 jit_solution(11837743213971884637)
XLA Ops:
  1.3 0.0 copy-start.3
  1.9 0.0 copy-done.3
  2.0 0.1 copy.9.pos_ref
  2.1 0.0 copy-start
  2.1 1.2 %copy-done = bf16[128,4096]{1,0:T(8,128)(2,1)S(1)} copy-done((bf16[128,4096]{1,0:T(8,128)(2,1)S(1)}, bf16[128,4096]{1,0:T(8,128)(2,1)}, u32[]{:S(2)}) %copy-start) | copy-done | bytes 1048600
  3.3 0.0 copy-start.1
  3.3 0.9 %copy-done.1 = bf16[256,384]{1,0:T(8,128)(2,1)S(1)} copy-done((bf16[256,384]{1,0:T(8,128)(2,1)S(1)}, bf16[256,384]{1,0:T(8,128)(2,1)}, u32[]{:S(2)}) %copy-start.1) | copy-done | bytes 196632
  4.2 0.0 copy-start.2
  4.2 0.9 %copy-done.2 = bf16[128,384]{1,0:T(8,128)(2,1)S(1)} copy-done((bf16[128,384]{1,0:T(8,128)(2,1)S(1)}, bf16[128,384]{1,0:T(8,128)(2,1)}, u32[]{:S(2)}) %copy-start.2) | copy-done | bytes 98328
  5.1 59.0 %shard_map.85 = (f32[1,128]{1,0:T(1,128)S(1)}, f32[256,384]{1,0:T(8,128)S(1)}, f32[2]{0:T(128)S(1)}) custom-call(bf16[128,4096]{1,0:T(8,128)(2,1)S(1)} %copy-done, bf16[256,384]{1,0:T(8,128)(2,1)S(1)} %copy-done.1, bf16[128,384]{1,0:T(8,128)(2,1)S(1)} %copy-done.2, f32[1]{0:T(128)S(6)} %copy.13.ls_ref, f32[1]{0:T(128)S(6)} %copy.14.bias_ref, ...), custom_call_target="tpu_custom_call" | custom-call | flops 1300000000 | bytes 3000000 | tf_op jit(solution)/shard_map/pallas_call | solution.py:327
  64.2 0.5 copy.15
  64.7 0.7 %copy.16 = f32[256,384]{1,0:T(8,128)} copy(f32[256,384]{1,0:T(8,128)S(1)} %get-tuple-element.13) | data formatting | bytes 786432
  65.4 0.5 copy.17
Async XLA Ops:
  1.3 0.7 %copy-start.3 = (s32[128,2]{0,1:T(2,128)S(1)}, s32[128,2]{0,1:T(2,128)}, u32[]{:S(2)}) copy-start(s32[128,2]{0,1:T(2,128)} %param.11) | copy-start | bytes 3076
  2.1 1.2 %copy-start = (bf16[128,4096]{1,0:T(8,128)(2,1)S(1)}, bf16[128,4096]{1,0:T(8,128)(2,1)}, u32[]{:S(2)}) copy-start(bf16[128,4096]{1,0:T(8,128)(2,1)} %clips_hbm.1) | copy-start | bytes 3145732
  3.3 0.9 %copy-start.1 = (bf16[256,384]{1,0:T(8,128)(2,1)S(1)}, bf16[256,384]{1,0:T(8,128)(2,1)}, u32[]{:S(2)}) copy-start(bf16[256,384]{1,0:T(8,128)(2,1)} %w_hbm.1) | copy-start | bytes 589828
  4.2 0.9 %copy-start.2 = (bf16[128,384]{1,0:T(8,128)(2,1)S(1)}, bf16[128,384]{1,0:T(8,128)(2,1)}, u32[]{:S(2)}) copy-start(bf16[128,384]{1,0:T(8,128)(2,1)} %s_hbm.1) | copy-start | bytes 294916
